TPU v7x, 32 devices: a whole 2x2x4 slice. The times are simulated.
32 devices in a mesh: section: 2 (over x), expert: 4 (over z), tensor: 4 (over y, core).
Axes of the slice: x: 2, y: 2, z: 4, core: 2. Of those that a mesh axis runs over, the one named last changes fastest.
Arguments:
- slab: bfloat16 [2, 768, 7168], P('section', ('expert', 'tensor')), may hold values from -6 to 6
- route_ids: int32 [2, 768, 2], P('section', ('expert', 'tensor')), may hold values from 0 to 3, all different within a row; in each aligned block of 48 rows (0 to 47, 48 to 95, ..., all dimensions but the last counted through in order) at most 48 rows name the same one
- route_weights: float32 [2, 768, 2], P('section', ('expert', 'tensor')), may hold values from 0.1 to 1
- norm_gain: float32 [2, 7168], P('section'), may hold values from 0.25 to 1.75
- w_gate: bfloat16 [2, 4, 7168, 1024], P('section', 'expert', None, 'tensor'), may hold values from -0.0625 to 0.0625
- w_up: bfloat16 [2, 4, 7168, 1024], P('section', 'expert', None, 'tensor'), may hold values from -0.0625 to 0.0625
- w_down: bfloat16 [2, 4, 1024, 7168], P('section', 'expert', 'tensor'), may hold values from -0.1875 to 0.1875
Outputs:
- next_slab: bfloat16 [2, 768, 7168], P('section', ('expert', 'tensor'))
Inputs may be any that keep to these rules, and one draw needn't show every extreme that they name: `route_ids`: within the rows of one device (aligned blocks of 48 token rows) no expert is named by more than 48 rows, a bound that some block reaches. The ids of a row differ.
All inputs are finite; a program needn't handle non-finite values.
Results may differ from a plain program's by a relative error of at most 0.006.
Values may be sent and summed in bfloat16 or wider, within the bound.
A program may use at most 128 MiB of HBM per device.

v0:
```python
import jax
import jax.numpy as jnp
from jax import lax
from jax.sharding import PartitionSpec as P


def from_behind(block, axis, distance):
    devices = range(lax.axis_size(axis))
    route = [((i - distance) % len(devices), i) for i in devices]
    return lax.ppermute(block, axis, route)


def rms_normed(rows, gain):
    values = rows.astype(jnp.float32)
    scale = lax.rsqrt(jnp.mean(values * values, axis=-1, keepdims=True) + 1e-06)
    return (values * scale * gain).astype(jnp.bfloat16)


def local(slab, route_ids, route_weights, norm_gain, w_gate, w_up, w_down):
    arriving = from_behind(slab, "section", 1)
    rows = arriving[0]
    tokens_here = rows.shape[0]
    width = rows.shape[1]
    owners = lax.axis_size("expert")
    groups = lax.axis_size("tensor")
    chosen = route_ids.shape[2]
    capacity = 2 * tokens_here * chosen // owners
    normed = rms_normed(rows, norm_gain[0])
    ids = route_ids[0].reshape(-1)
    onehot = (ids[:, None] == jnp.arange(owners, dtype=jnp.int32)[None, :]).astype(jnp.int32)
    rank = jnp.sum((jnp.cumsum(onehot, axis=0) - onehot) * onehot, axis=1)
    slot_key = ids * capacity + rank
    placing = jnp.arange(owners * capacity, dtype=jnp.int32)[:, None] == slot_key[None, :]
    place_tok = jnp.any(placing.reshape(owners * capacity, tokens_here, chosen), axis=2).astype(
        jnp.bfloat16
    )
    buffer = jnp.dot(place_tok, normed, preferred_element_type=jnp.float32).astype(jnp.bfloat16)
    buffer = buffer.reshape(owners, capacity, width)
    gate_w = w_gate[0, 0]
    up_w = w_up[0, 0]
    down_w = w_down[0, 0]
    slice_width = gate_w.shape[1]
    received = lax.all_to_all(buffer, "expert", split_axis=0, concat_axis=0, tiled=True)
    block = lax.all_gather(received[None], "tensor", axis=0, tiled=True)
    flat = block.reshape(-1, width)
    gate = jnp.dot(flat, gate_w, preferred_element_type=jnp.float32)
    up = jnp.dot(flat, up_w, preferred_element_type=jnp.float32)
    hidden = (jax.nn.silu(gate) * up).astype(jnp.bfloat16)
    hidden = hidden.reshape(block.shape[:-1] + (slice_width,))
    flat_hidden = hidden.reshape(groups * owners * capacity, slice_width)
    summed = lax.psum_scatter(
        jnp.dot(flat_hidden, down_w, preferred_element_type=jnp.float32).astype(jnp.bfloat16),
        "tensor",
        scatter_dimension=0,
        tiled=True,
    )
    outgoing = summed.reshape(owners, capacity, width)
    back = lax.all_to_all(outgoing, "expert", split_axis=0, concat_axis=0, tiled=True)
    picked = back.reshape(owners * capacity, width)[slot_key].astype(jnp.float32)
    weighted = picked * route_weights[0].reshape(-1)[:, None]
    mixed = jnp.sum(weighted.reshape(tokens_here, chosen, width), axis=1)
    return (rows.astype(jnp.float32) + mixed).astype(jnp.bfloat16)[None]


def solution(mesh):
    return jax.shard_map(
        local,
        mesh=mesh,
        in_specs=(
            P("section", ("expert", "tensor"), None),
            P("section", ("expert", "tensor"), None),
            P("section", ("expert", "tensor"), None),
            P("section", None),
            P("section", "expert", None, "tensor"),
            P("section", "expert", None, "tensor"),
            P("section", "expert", "tensor", None),
        ),
        out_specs=P("section", ("expert", "tensor"), None),
        check_vma=False,
    )
```

profile of v0, /device:TPU:0, one launch (start us, length us, event | category | flops | bytes accessed | tf_op | source)
XLA Modules:
  0.0 364.6 jit_solution(376999290803715111)
XLA Ops:
  6.5 0.0 all-gather.3.cloned.1.call-start
  6.5 2.9 collective-permute-start
  9.5 0.8 copy.23
  10.2 0.1 eq.30
  10.4 0.1 fusion.29
  10.5 0.1 reduce_window_sum.11
  10.6 0.2 select_reduce_fusion
  10.8 0.1 reduce_sum.34
  10.9 0.1 copy.24
  11.0 0.7 bitcast_add_fusion
  11.7 0.1 fusion.28
  11.8 13.4 %collective-permute-done = bf16[1,48,7168]{2,1,0:T(8,128)(2,1)S(1)} collective-permute-done((bf16[1,48,7168]{2,1,0:T(8,128)(2,1)}, bf16[1,48,7168]{2,1,0:T(8,128)(2,1)S(1)}, u32[]{:S(2)}, u32[]{:S(2)}) %collective-permute-start) | collective-permute-done | bytes 688160 | tf_op jit(solution)/shard_map/ppermute | solution.py:10
  25.1 0.3 fusion.7
  25.4 1.7 convolution_convert_fusion.1
  27.1 66.4 %all_to_all.10 = bf16[4,48,7168]{2,1,0:T(8,128)(2,1)} all-to-all(bf16[4,48,7168]{2,1,0:T(8,128)(2,1)S(1)} %bitcast.50), channel_id=1, replica_groups=mesh['section'=2,'expert'=4,'tensor'=4] {'expert'}, dimensions={0} | all-to-all | bytes 5505024 | tf_op jit(solution)/shard_map/all_to_all | solution.py:43
  93.5 0.0 all-gather.3.cloned.1.call-update
  93.5 0.0 reduce-scatter.2.cloned.1.call-start
  93.6 72.4 %all-gather.3.cloned.1.call-done = bf16[16,48,7168]{2,1,0:T(8,128)(2,1)} async-done(((bf16[4,48,7168]{2,1,0:T(8,128)(2,1)}), bf16[16,48,7168]{2,1,0:T(8,128)(2,1)}) %all-gather.3.cloned.1.call-update) | async-done | bytes 11010064 | tf_op jit(solution)/shard_map/all_gather | solution.py:44
  166.0 6.9 %fusion.3 = f32[768,256]{1,0:T(8,128)S(1)} fusion(bf16[768,7168]{1,0:T(8,128)(2,1)} %bitcast.48, bf16[1,1,7168,256]{3,2,1,0:T(8,128)(2,1)} %param.11), kind=kOutput, calls=%fused_computation.6 | convolution fusion | flops 2818572288 | bytes 15466496 | tf_op jit(solution)/shard_map/dot_general | solution.py:46
  172.8 18.9 %convolution_convert_fusion = bf16[768,7168]{1,0:T(8,128)(2,1)} fusion(bf16[1,1,256,7168]{3,2,1,0:T(8,128)(2,1)} %param.13, bf16[768,7168]{1,0:T(8,128)(2,1)} %bitcast.49, bf16[1,1,7168,256]{3,2,1,0:T(8,128)(2,1)} %param.12, f32[768,256]{1,0:T(8,128)S(1)} %fusion.3), kind=kOutput, calls=%fused_computation.1 | convolution fusion | flops 5643829248 | bytes 30146560 | tf_op jit(solution)/shard_map/dot_general | solution.py:52
  191.7 0.0 reduce-scatter.2.cloned.1.call-update
  191.7 88.9 %reduce-scatter.2.cloned.1.call-done = bf16[192,7168]{1,0:T(8,128)(2,1)} async-done(((bf16[768,7168]{1,0:T(8,128)(2,1)}), bf16[192,7168]{1,0:T(8,128)(2,1)}) %reduce-scatter.2.cloned.1.call-update) | async-done | bytes 2752528 | tf_op jit(solution)/shard_map/reduce_scatter | solution.py:51
  280.6 0.0 copy-start
  280.6 0.0 copy-start.1
  280.6 4.7 %all-to-all-start.1 = ((bf16[4,48,7168]{2,1,0:T(8,128)(2,1)}), bf16[4,48,7168]{2,1,0:T(8,128)(2,1)S(1)}, u32[]{:S(2)}, u32[]{:S(2)}) async-start(bf16[4,48,7168]{2,1,0:T(8,128)(2,1)} %bitcast.51), calls=%async_computation.2 | async-start | bytes 5505024 | tf_op jit(solution)/shard_map/all_to_all | solution.py:58
  285.4 0.0 copy-done
  285.4 0.1 copy.25
  285.5 0.1 mul.77
  285.6 0.0 copy-done.1
  285.6 0.1 copy.26
  285.7 61.9 %all-to-all-done.1 = bf16[4,48,7168]{2,1,0:T(8,128)(2,1)S(1)} async-done(((bf16[4,48,7168]{2,1,0:T(8,128)(2,1)}), bf16[4,48,7168]{2,1,0:T(8,128)(2,1)S(1)}, u32[]{:S(2)}, u32[]{:S(2)}) %all-to-all-start.1) | async-done | bytes 2752544 | tf_op jit(solution)/shard_map/all_to_all | solution.py:58
  347.6 2.5 gather_fusion
  350.1 3.1 reshape.87
  353.2 3.6 multiply_reduce_fusion
  356.8 1.0 fusion.10
  (4 shorter events, 0.0 us)
Async XLA Ops:
  6.5 159.4 %all-gather.3.cloned.1.call-start = ((), (), s32[]{:S(2)}) async-start(), calls=%async_computation.4 | async-start | bytes 13762560 | tf_op jit(solution)/shard_map/all_gather | solution.py:44
  6.5 18.6 %collective-permute-start = (bf16[1,48,7168]{2,1,0:T(8,128)(2,1)}, bf16[1,48,7168]{2,1,0:T(8,128)(2,1)S(1)}, u32[]{:S(2)}, u32[]{:S(2)}) collective-permute-start(bf16[1,48,7168]{2,1,0:T(8,128)(2,1)} %param.7), channel_id=1, source_target_pairs={{16,0},{0,16},{17,1},{1,17},{18,2},{2,18},{19,3},{3,19},{20,4},{4,... | collective-permute-start | bytes 2064392 | tf_op jit(solution)/shard_map/ppermute | solution.py:10
  93.5 187.1 %reduce-scatter.2.cloned.1.call-start = ((), (), s32[]{:S(2)}) async-start(), calls=%async_computation.3 | async-start | bytes 13762560 | tf_op jit(solution)/shard_map/reduce_scatter | solution.py:51
  280.6 4.7 %copy-start = (s32[1,48,2]{1,2,0:T(2,128)S(1)}, s32[1,48,2]{1,2,0:T(2,128)}, u32[]{:S(2)}) copy-start(s32[1,48,2]{1,2,0:T(2,128)} %param.8) | copy-start | bytes 1156
  280.6 5.0 %copy-start.1 = (f32[1,48,2]{1,2,0:T(2,128)S(1)}, f32[1,48,2]{1,2,0:T(2,128)}, u32[]{:S(2)}) copy-start(f32[1,48,2]{1,2,0:T(2,128)} %param.9) | copy-start | bytes 1156
  280.6 67.0 %all-to-all-start.1 = ((bf16[4,48,7168]{2,1,0:T(8,128)(2,1)}), bf16[4,48,7168]{2,1,0:T(8,128)(2,1)S(1)}, u32[]{:S(2)}, u32[]{:S(2)}) async-start(bf16[4,48,7168]{2,1,0:T(8,128)(2,1)} %bitcast.51), calls=%async_computation.2 | async-start | bytes 5505024 | tf_op jit(solution)/shard_map/all_to_all | solution.py:58
Sparse Core Ops, SparseCore 0:
  93.6 72.2 all-gather.2
  191.9 88.7 reduce-scatter.1
where the time goes:
time: 365 us
  waiting for transfers between devices  237 us (65%)
  blocking collectives  66.4 us (18%)
  matrix products  27.4 us (8%)
  between operations  13.5 us (4%)
  starting transfers between devices  7.71 us (2%)
  local copies, waits for them, and re-layouts  7 us (2%)
  other arithmetic  6.02 us (2%)
    reduce_scatter x1, waiting for transfers between devices, local(): lax.psum_scatter(jnp.dot(flat_hidden, down_w, preferred_element_type=jnp....  88.9 us
    all_gather x1, waiting for transfers between devices, local(): block = lax.all_gather(received[None], 'tensor', axis=0, tiled=True)  72.4 us
    all_to_all x1, blocking collectives, local(): lax.all_to_all(buffer, 'expert', split_axis=0, concat_axis=0, tiled=True)  66.4 us
    all_to_all x1, waiting for transfers between devices, local(): lax.all_to_all(outgoing, 'expert', split_axis=0, concat_axis=0, tiled=True)  61.9 us
    dot_general x1, matrix products, local(): jnp.dot(flat_hidden, down_w, preferred_element_type=jnp.float32)  18.9 us
    ppermute x1, waiting for transfers between devices, from_behind(): return lax.ppermute(block, axis, route)  13.4 us
  transfers between devices with their start and end apart: 4, of which 4 were waited for; matrix products, arithmetic and copies ran while one was open for 1% of the time, Pallas kernels for 0%

commit v1 on v0

v1 whole, which is shorter than its diff:
```python
import functools

import jax
import jax.numpy as jnp
from jax import lax
from jax.experimental import pallas as pl
from jax.experimental.pallas import tpu as pltpu
from jax.sharding import PartitionSpec as P

MESH = pl.DeviceIdType.MESH
CHUNK = 16
PAD = 128
CORES = 2


def kernel(
    sizes,
    slab_ref,
    ids_ref,
    rw_ref,
    gain_ref,
    wg_ref,
    wu_ref,
    wd_ref,
    out_ref,
    xbuf,
    tok,
    wgs,
    wus,
    wds,
    hid,
    part,
    yrecv,
    zrecv,
    x_send,
    x_recv,
    w_local,
    w_send,
    w_recv,
    t_right,
    t_left,
    t_y,
    t_recv,
    p_y,
    p_yrecv,
    p_z,
    p_zrecv,
):
    sections, owners, groups = sizes
    rows, width = out_ref.shape
    chunks = rows // CHUNK
    section = lax.axis_index("section")
    z = lax.axis_index("expert")
    t = lax.axis_index("tensor")
    core = lax.rem(t, CORES)
    y = t // CORES
    other_y = 1 - y
    mate = {"tensor": y * CORES + 1 - core}
    across = {"tensor": other_y * CORES + core}
    ahead = {"section": lax.rem(section + 1, sections)}
    behind = {"section": lax.rem(section + sections - 1, sections)}
    right = {"expert": lax.rem(z + 1, owners)}
    left = {"expert": lax.rem(z + owners - 1, owners)}
    has_right = z < owners - 1
    has_left = z > 0

    def remote(src, dst, send, recv, where):
        return pltpu.make_async_remote_copy(
            src_ref=src,
            dst_ref=dst,
            send_sem=send,
            recv_sem=recv,
            device_id=where,
            device_id_type=MESH,
        )

    def lines(k, side=None):
        if side is None:
            return pl.ds(k * CHUNK, CHUNK)
        return pl.ds(pl.multiple_of(side * rows + k * CHUNK, CHUNK), CHUNK)

    barrier = pltpu.get_barrier_semaphore()
    for where in (mate, across, ahead, behind):
        pl.semaphore_signal(barrier, inc=1, device_id=where, device_id_type=MESH)

    @pl.when(has_right)
    def _():
        pl.semaphore_signal(barrier, inc=1, device_id=right, device_id_type=MESH)

    @pl.when(has_left)
    def _():
        pl.semaphore_signal(barrier, inc=1, device_id=left, device_id_type=MESH)

    edge = jnp.where(has_right, 1, 0) + jnp.where(has_left, 1, 0)
    pl.semaphore_wait(barrier, 4 + edge)

    def x_copy(k):
        return remote(
            slab_ref.at[lines(k)], xbuf.at[lines(k)], x_send.at[k], x_recv.at[k], ahead
        )

    for k in range(chunks):
        x_copy(k).start()

    weights = ((wg_ref, wgs), (wu_ref, wus), (wd_ref, wds))

    def w_copies(i):
        source, target = weights[i]
        return (
            pltpu.make_async_copy(source, target.at[core], w_local.at[i]),
            remote(source, target.at[core], w_send.at[i], w_recv.at[i], mate),
        )

    for i in range(3):
        for copy in w_copies(i):
            copy.start()

    def t_copy(zs, k, sends, where):
        place = tok.at[zs, lines(k, y)]
        return remote(place, place, sends.at[zs, k], t_recv.at[y, zs, k], where)

    def t_arrived(zs, side, k):
        place = tok.at[zs, lines(k, side)]
        return remote(place, place, t_y.at[zs, k], t_recv.at[side, zs, k], across)

    lane = lax.broadcasted_iota(jnp.int32, (CHUNK, PAD), 1)
    for k in range(chunks):
        x_copy(k).wait_recv()
        values = xbuf[lines(k)].astype(jnp.float32)
        scale = lax.rsqrt(jnp.mean(values * values, axis=-1, keepdims=True) + 1e-06)
        tok[z, lines(k, y), 0:width] = (values * scale * gain_ref[...]).astype(
            jnp.bfloat16
        )
        expert = lax.rem(lane, owners)
        dense = jnp.zeros((CHUNK, PAD), jnp.float32)
        for c in range(ids_ref.shape[1]):
            hit = expert == ids_ref[lines(k), c : c + 1]
            dense = jnp.where(hit, rw_ref[lines(k), c : c + 1], dense)
        high = dense.astype(jnp.bfloat16).astype(jnp.float32)
        rest = dense - high
        middle = rest.astype(jnp.bfloat16).astype(jnp.float32)
        low = rest - middle
        third = lane // owners
        packed = jnp.where(
            third == 0,
            high,
            jnp.where(third == 1, middle, jnp.where(third == 2, low, 0.0)),
        )
        tok[z, lines(k, y), width : width + PAD] = packed.astype(jnp.bfloat16)

        @pl.when(has_right)
        def _():
            t_copy(z, k, t_right, right).start()

        @pl.when(has_left)
        def _():
            t_copy(z, k, t_left, left).start()

        t_copy(z, k, t_y, across).start()

    def at(j):
        return z + ((j + 1) // 2) * (1 - 2 * lax.rem(j, 2))

    def inside(zs):
        return jnp.logical_and(zs >= 0, zs < owners)

    def forward(zs):
        for k in range(chunks):
            t_arrived(zs, y, k).wait_recv()

            @pl.when(jnp.logical_and(zs < z, has_right))
            def _():
                t_copy(zs, k, t_right, right).start()

            @pl.when(jnp.logical_and(zs > z, has_left))
            def _():
                t_copy(zs, k, t_left, left).start()

            t_copy(zs, k, t_y, across).start()

    tall = 2 * rows
    hidden_width = wgs.shape[2]
    tile = width // 7 if width % (7 * 128) == 0 else 128

    def compute(zs):
        for k in range(chunks):
            t_arrived(zs, other_y, k).wait_recv()
        for h in range(CORES):
            gate = jnp.dot(
                tok[zs, :, 0:width], wgs[h], preferred_element_type=jnp.float32
            )
            up = jnp.dot(
                tok[zs, :, 0:width], wus[h], preferred_element_type=jnp.float32
            )
            hid[:, h * hidden_width : (h + 1) * hidden_width] = (
                jax.nn.silu(gate) * up
            ).astype(jnp.bfloat16)
        spot = lax.broadcasted_iota(jnp.int32, (tall, PAD), 1)
        mine = jnp.logical_and(lax.rem(spot, owners) == z, spot < 3 * owners)
        share = jnp.sum(
            jnp.where(mine, tok[zs, :, width : width + PAD].astype(jnp.float32), 0.0),
            axis=1,
            keepdims=True,
        )

        def down(i, carry):
            span = pl.ds(pl.multiple_of(i * tile, 128), tile)
            product = jnp.dot(
                hid[:, 0:hidden_width],
                wds[0, :, span],
                preferred_element_type=jnp.float32,
            ) + jnp.dot(
                hid[:, hidden_width : 2 * hidden_width],
                wds[1, :, span],
                preferred_element_type=jnp.float32,
            )
            part[zs, :, span] = (product * share).astype(jnp.bfloat16)
            return carry

        lax.fori_loop(0, width // tile, down, 0)

    def gather_step(j, carry):
        zs = at(j)

        @pl.when(jnp.logical_and(j < 2 * owners - 1, inside(zs)))
        def _():
            forward(zs)

        before = at(j - 2)

        @pl.when(j == 2)
        def _():
            for i in range(3):
                local_copy, mate_copy = w_copies(i)
                local_copy.wait()
                remote(
                    weights[i][0],
                    weights[i][1].at[1 - core],
                    w_send.at[i],
                    w_recv.at[i],
                    mate,
                ).wait_recv()

        @pl.when(jnp.logical_and(j >= 2, inside(before)))
        def _():
            compute(before)

        return carry

    lax.fori_loop(1, 2 * owners + 1, gather_step, 0)

    def y_copy(zs, k):
        return remote(
            part.at[zs, lines(k, other_y)],
            yrecv.at[zs, lines(k)],
            p_y.at[zs, k],
            p_yrecv.at[zs, k],
            across,
        )

    def z_copy(zs, slot, k, where):
        return remote(
            part.at[zs, lines(k, y)],
            zrecv.at[slot, lines(k)],
            p_z.at[zs, k],
            p_zrecv.at[slot, k],
            where,
        )

    def send_y(i, carry):
        zs = at(2 * owners - 2 - i)

        @pl.when(inside(zs))
        def _():
            for k in range(chunks):
                y_copy(zs, k).start()

        return carry

    lax.fori_loop(0, 2 * owners - 1, send_y, 0)

    def reduce_step(i, carry):
        zs = at(2 * owners - 2 - i)

        @pl.when(inside(zs))
        def _():
            for k in range(chunks):
                y_copy(zs, k).wait_recv()
                where = (zs, lines(k, y))
                both = part[where].astype(jnp.float32) + yrecv[zs, lines(k)].astype(
                    jnp.float32
                )
                outer = jnp.logical_or(
                    jnp.logical_and(zs > z, has_left),
                    jnp.logical_and(zs < z, has_right),
                )

                @pl.when(outer)
                def _():
                    z_copy(zs, zs, k, right).wait_recv()
                    part[where] = (
                        both + zrecv[zs, lines(k)].astype(jnp.float32)
                    ).astype(jnp.bfloat16)

                @pl.when(jnp.logical_not(outer))
                def _():
                    part[where] = both.astype(jnp.bfloat16)

                @pl.when(zs > z)
                def _():
                    z_copy(zs, zs, k, right).start()

                @pl.when(zs < z)
                def _():
                    slot = jnp.where(zs == z - 1, owners, zs)
                    z_copy(zs, slot, k, left).start()

        return carry

    lax.fori_loop(0, 2 * owners - 2, reduce_step, 0)

    for k in range(chunks):
        y_copy(z, k).wait_recv()
        total = (
            xbuf[lines(k)].astype(jnp.float32)
            + part[z, lines(k, y)].astype(jnp.float32)
            + yrecv[z, lines(k)].astype(jnp.float32)
        )
        hid_zero = jnp.zeros((CHUNK, width), jnp.bfloat16)

        @pl.when(has_left)
        def _():
            z_copy(z, z, k, right).wait_recv()

        @pl.when(jnp.logical_not(has_left))
        def _():
            zrecv[z, lines(k)] = hid_zero

        @pl.when(has_right)
        def _():
            z_copy(z, owners, k, left).wait_recv()

        @pl.when(jnp.logical_not(has_right))
        def _():
            zrecv[owners, lines(k)] = hid_zero

        total = total + (
            zrecv[z, lines(k)].astype(jnp.float32)
            + zrecv[owners, lines(k)].astype(jnp.float32)
        )
        out_ref[lines(k)] = total.astype(jnp.bfloat16)

    for k in range(chunks):
        x_copy(k).wait_send()
    for i in range(3):
        w_copies(i)[1].wait_send()

    def settle(zs, carry):
        for k in range(chunks):
            t_copy(zs, k, t_y, across).wait_send()
            y_copy(zs, k).wait_send()

            @pl.when(jnp.logical_and(zs <= z, has_right))
            def _():
                t_copy(zs, k, t_right, right).wait_send()

            @pl.when(jnp.logical_and(zs >= z, has_left))
            def _():
                t_copy(zs, k, t_left, left).wait_send()

            @pl.when(zs != z)
            def _():
                z_copy(zs, zs, k, right).wait_send()

        return carry

    lax.fori_loop(0, owners, settle, 0)


def solution(mesh):
    sizes = (mesh.shape["section"], mesh.shape["expert"], mesh.shape["tensor"])

    def local(slab, route_ids, route_weights, norm_gain, w_gate, w_up, w_down):
        owners = sizes[1]
        rows, width = slab.shape[1:]
        hidden = w_gate.shape[3]
        chunks = rows // CHUNK
        tall = 2 * rows
        vmem = pl.BlockSpec(memory_space=pltpu.VMEM)
        hbm = pl.BlockSpec(memory_space=pl.ANY)
        dma = pltpu.SemaphoreType.DMA
        flops = 2 * owners * tall * width * hidden * 2 * 3
        out = pl.pallas_call(
            functools.partial(kernel, sizes),
            out_shape=jax.ShapeDtypeStruct((rows, width), jnp.bfloat16),
            in_specs=[hbm, vmem, vmem, vmem, hbm, hbm, hbm],
            out_specs=vmem,
            scratch_shapes=[
                pltpu.VMEM((rows, width), jnp.bfloat16),
                pltpu.VMEM((owners, tall, width + PAD), jnp.bfloat16),
                pltpu.VMEM((CORES, width, hidden), jnp.bfloat16),
                pltpu.VMEM((CORES, width, hidden), jnp.bfloat16),
                pltpu.VMEM((CORES, hidden, width), jnp.bfloat16),
                pltpu.VMEM((tall, CORES * hidden), jnp.bfloat16),
                pltpu.VMEM((owners, tall, width), jnp.bfloat16),
                pltpu.VMEM((owners, rows, width), jnp.bfloat16),
                pltpu.VMEM((owners + 1, rows, width), jnp.bfloat16),
                dma((chunks,)),
                dma((chunks,)),
                dma((3,)),
                dma((3,)),
                dma((3,)),
                dma((owners, chunks)),
                dma((owners, chunks)),
                dma((owners, chunks)),
                dma((2, owners, chunks)),
                dma((owners, chunks)),
                dma((owners, chunks)),
                dma((owners, chunks)),
                dma((owners + 1, chunks)),
            ],
            compiler_params=pltpu.CompilerParams(
                collective_id=0,
                has_side_effects=True,
                vmem_limit_bytes=60 * 1024 * 1024,
            ),
            cost_estimate=pl.CostEstimate(
                flops=flops,
                bytes_accessed=12 * width * hidden,
                transcendentals=owners * tall * hidden * 2,
            ),
        )(
            slab[0],
            route_ids[0],
            route_weights[0],
            norm_gain,
            w_gate[0, 0],
            w_up[0, 0],
            w_down[0, 0],
        )
        return out[None]

    return jax.shard_map(
        local,
        mesh=mesh,
        in_specs=(
            P("section", ("expert", "tensor"), None),
            P("section", ("expert", "tensor"), None),
            P("section", ("expert", "tensor"), None),
            P("section", None),
            P("section", "expert", None, "tensor"),
            P("section", "expert", None, "tensor"),
            P("section", "expert", "tensor", None),
        ),
        out_specs=P("section", ("expert", "tensor"), None),
        check_vma=False,
    )
```

time: 365 us -> 143 us (0.39)
  waiting for transfers between devices: 237 us -> 0 us
  Pallas kernels: 0 us -> 138 us
  blocking collectives: 66.4 us -> 0 us
  matrix products: 27.4 us -> 0 us
  between operations: 13.5 us -> 0.01 us
  starting transfers between devices: 7.71 us -> 0 us
  other arithmetic: 6.02 us -> 0 us
    pallas_call x0 -> x1, Pallas kernels: none -> 138 us  [local(): pl.pallas_call(functools.partial(kernel, sizes), out_shape=jax.ShapeDtype...]
    reduce_scatter x1 -> x0, waiting for transfers between devices: 88.9 us -> none  [local(): lax.psum_scatter(jnp.dot(flat_hidden, down_w, preferred_element_type=jnp....]
    all_gather x1 -> x0, waiting for transfers between devices: 72.4 us -> none  [local(): block = lax.all_gather(received[None], 'tensor', axis=0, tiled=True)]
    all_to_all x1 -> x0, blocking collectives: 66.4 us -> none  [local(): lax.all_to_all(buffer, 'expert', split_axis=0, concat_axis=0, tiled=True)]
    all_to_all x1 -> x0, waiting for transfers between devices: 61.9 us -> none  [local(): lax.all_to_all(outgoing, 'expert', split_axis=0, concat_axis=0, tiled=True)]
    dot_general x3 -> x0, matrix products: 27.4 us -> none  [the longest x1 18.9 us: local(): jnp.dot(flat_hidden, down_w, preferred_element_type=jnp.float32)]
    ppermute x1 -> x0, waiting for transfers between devices: 13.4 us -> none  [from_behind(): return lax.ppermute(block, axis, route)]
    all_to_all x1 -> x0, starting transfers between devices: 4.73 us -> none  [local(): lax.all_to_all(outgoing, 'expert', split_axis=0, concat_axis=0, tiled=True)]
  transfers between devices with their start and end apart: 4 -> 0, of which waited for: 4 -> 0; matrix products, arithmetic and copies ran while one was open for 1% -> 0% of each run, Pallas kernels for 0% -> 0%
where the time goes in v1:
time: 143 us
  Pallas kernels  138 us (97%)
  local copies, waits for them, and re-layouts  4.73 us (3%)
    pallas_call x1, Pallas kernels, local(): pl.pallas_call(functools.partial(kernel, sizes), out_shape=jax.ShapeDtype...  138 us

profile of v1, /device:TPU:0, one launch (start us, length us, event | category | flops | bytes accessed | tf_op | source)
XLA Modules:
  0.0 142.8 jit_solution(3222612976585597083)
XLA Ops:
  0.0 1.4 copy.8.ids_ref
  1.4 1.4 copy.9.rw_ref
  2.7 138.0 %shard_map.73 = bf16[48,7168]{1,0:T(8,128)(2,1)} custom-call(bf16[48,7168]{1,0:T(8,128)(2,1)} %bitcast.13, s32[48,2]{1,0:T(8,128)} %copy.8.ids_ref, f32[48,2]{1,0:T(8,128)} %copy.9.rw_ref, f32[1,7168]{1,0:T(1,128)} %gain_ref.1, bf16[7168,256]{1,0:T(8,128)(2,1)} %bitcast.10, bf16[7168,256]{1,0:T(8,128)(2,1)} %bitcast.11, bf16[256,7168]{1,0:T(8,128)(2,1)} %bitcast.12), custom_call_target="tpu_custom_call" | custom-call | flops 8455716864 | bytes 22020096 | tf_op jit(solution)/shard_map/pallas_call | solution.py:393
  140.8 2.0 %copy.11 = bf16[1,48,7168]{2,1,0:T(8,128)(2,1)} copy(bf16[1,48,7168]{2,1,0:T(8,128)(2,1)} %bitcast.7) | data formatting | bytes 1376256

commit v2 on v1

--- a/solution.py
+++ b/solution.py
@@ -16,8 +16,7 @@
 def kernel(
     sizes,
     slab_ref,
-    ids_ref,
-    rw_ref,
+    dense_ref,
     gain_ref,
     wg_ref,
     wu_ref,
@@ -45,10 +44,19 @@
     p_yrecv,
     p_z,
     p_zrecv,
+    brecv,
+    bown,
+    b_right,
+    b_left,
+    b_recv,
+    pb_z,
+    pb_recv,
+    last,
 ):
     sections, owners, groups = sizes
     rows, width = out_ref.shape
     chunks = rows // CHUNK
+    first = yrecv.shape[2]
     section = lax.axis_index("section")
     z = lax.axis_index("expert")
     t = lax.axis_index("tensor")
@@ -123,6 +131,25 @@
         place = tok.at[zs, lines(k, side)]
         return remote(place, place, t_y.at[zs, k], t_recv.at[side, zs, k], across)
 
+    def a_copy(zs, side, k):
+        place = tok.at[zs, lines(k, side), 0:first]
+        return remote(place, place, t_y.at[zs, k], t_recv.at[side, zs, k], across)
+
+    other_rows = pl.ds(pl.multiple_of(other_y * rows, CHUNK), rows)
+
+    def b_copy(zs, sends, where):
+        place = tok.at[zs, other_rows, first : width + PAD]
+        return remote(place, place, sends.at[zs], b_recv.at[zs], where)
+
+    def b_spread(zs, to_right, to_left):
+        @pl.when(to_right)
+        def _():
+            b_copy(zs, b_right, right).start()
+
+        @pl.when(to_left)
+        def _():
+            b_copy(zs, b_left, left).start()
+
     lane = lax.broadcasted_iota(jnp.int32, (CHUNK, PAD), 1)
     for k in range(chunks):
         x_copy(k).wait_recv()
@@ -131,11 +158,7 @@
         tok[z, lines(k, y), 0:width] = (values * scale * gain_ref[...]).astype(
             jnp.bfloat16
         )
-        expert = lax.rem(lane, owners)
-        dense = jnp.zeros((CHUNK, PAD), jnp.float32)
-        for c in range(ids_ref.shape[1]):
-            hit = expert == ids_ref[lines(k), c : c + 1]
-            dense = jnp.where(hit, rw_ref[lines(k), c : c + 1], dense)
+        dense = dense_ref[lines(k)]
         high = dense.astype(jnp.bfloat16).astype(jnp.float32)
         rest = dense - high
         middle = rest.astype(jnp.bfloat16).astype(jnp.float32)
@@ -158,6 +181,10 @@
 
         t_copy(z, k, t_y, across).start()
 
+    for k in range(chunks):
+        t_arrived(z, other_y, k).wait_recv()
+    b_spread(z, has_right, has_left)
+
     def at(j):
         return z + ((j + 1) // 2) * (1 - 2 * lax.rem(j, 2))
 
@@ -176,15 +203,24 @@
             def _():
                 t_copy(zs, k, t_left, left).start()
 
-            t_copy(zs, k, t_y, across).start()
+            a_copy(zs, y, k).start()
+        b_copy(zs, b_right, right).wait_recv()
+        b_spread(
+            zs,
+            jnp.logical_and(zs < z, has_right),
+            jnp.logical_and(zs > z, has_left),
+        )
 
     tall = 2 * rows
     hidden_width = wgs.shape[2]
     tile = width // 7 if width % (7 * 128) == 0 else 128
 
     def compute(zs):
-        for k in range(chunks):
-            t_arrived(zs, other_y, k).wait_recv()
+        @pl.when(zs != z)
+        def _():
+            for k in range(chunks):
+                a_copy(zs, other_y, k).wait_recv()
+
         for h in range(CORES):
             gate = jnp.dot(
                 tok[zs, :, 0:width], wgs[h], preferred_element_type=jnp.float32
@@ -251,7 +287,7 @@
 
     def y_copy(zs, k):
         return remote(
-            part.at[zs, lines(k, other_y)],
+            part.at[zs, lines(k, other_y), 0:first],
             yrecv.at[zs, lines(k)],
             p_y.at[zs, k],
             p_yrecv.at[zs, k],
@@ -267,6 +303,24 @@
             where,
         )
 
+    def c_copy(zs, slot, where):
+        return remote(
+            part.at[zs, other_rows, first:width],
+            brecv.at[slot],
+            pb_z.at[zs],
+            pb_recv.at[slot],
+            where,
+        )
+
+    def last_copy():
+        return remote(
+            part.at[z, other_rows, first:width],
+            bown,
+            last.at[0],
+            last.at[1],
+            across,
+        )
+
     def send_y(i, carry):
         zs = at(2 * owners - 2 - i)
 
@@ -284,27 +338,49 @@
 
         @pl.when(inside(zs))
         def _():
+            outer = jnp.logical_or(
+                jnp.logical_and(zs > z, has_left),
+                jnp.logical_and(zs < z, has_right),
+            )
+            slot = jnp.where(zs == z - 1, owners, zs)
+
+            @pl.when(outer)
+            def _():
+                c_copy(zs, zs, right).wait_recv()
+                part[zs, other_rows, first:width] = (
+                    part[zs, other_rows, first:width].astype(jnp.float32)
+                    + brecv[zs].astype(jnp.float32)
+                ).astype(jnp.bfloat16)
+
+            @pl.when(zs > z)
+            def _():
+                c_copy(zs, zs, right).start()
+
+            @pl.when(zs < z)
+            def _():
+                c_copy(zs, slot, left).start()
+
             for k in range(chunks):
                 y_copy(zs, k).wait_recv()
-                where = (zs, lines(k, y))
-                both = part[where].astype(jnp.float32) + yrecv[zs, lines(k)].astype(
-                    jnp.float32
-                )
-                outer = jnp.logical_or(
-                    jnp.logical_and(zs > z, has_left),
-                    jnp.logical_and(zs < z, has_right),
-                )
+                here = lines(k, y)
+                both = part[zs, here, 0:first].astype(jnp.float32) + yrecv[
+                    zs, lines(k)
+                ].astype(jnp.float32)
 
                 @pl.when(outer)
                 def _():
                     z_copy(zs, zs, k, right).wait_recv()
-                    part[where] = (
-                        both + zrecv[zs, lines(k)].astype(jnp.float32)
+                    part[zs, here, 0:first] = (
+                        both + zrecv[zs, lines(k), 0:first].astype(jnp.float32)
+                    ).astype(jnp.bfloat16)
+                    part[zs, here, first:width] = (
+                        part[zs, here, first:width].astype(jnp.float32)
+                        + zrecv[zs, lines(k), first:width].astype(jnp.float32)
                     ).astype(jnp.bfloat16)
 
                 @pl.when(jnp.logical_not(outer))
                 def _():
-                    part[where] = both.astype(jnp.bfloat16)
+                    part[zs, here, 0:first] = both.astype(jnp.bfloat16)
 
                 @pl.when(zs > z)
                 def _():
@@ -312,52 +388,86 @@
 
                 @pl.when(zs < z)
                 def _():
-                    slot = jnp.where(zs == z - 1, owners, zs)
                     z_copy(zs, slot, k, left).start()
 
         return carry
 
     lax.fori_loop(0, 2 * owners - 2, reduce_step, 0)
 
+    @pl.when(has_left)
+    def _():
+        c_copy(z, z, right).wait_recv()
+
+    @pl.when(jnp.logical_not(has_left))
+    def _():
+        brecv[z] = jnp.zeros(brecv.shape[1:], jnp.bfloat16)
+        zrecv[z] = jnp.zeros(zrecv.shape[1:], jnp.bfloat16)
+
+    @pl.when(has_right)
+    def _():
+        c_copy(z, owners, left).wait_recv()
+
+    @pl.when(jnp.logical_not(has_right))
+    def _():
+        brecv[owners] = jnp.zeros(brecv.shape[1:], jnp.bfloat16)
+        zrecv[owners] = jnp.zeros(zrecv.shape[1:], jnp.bfloat16)
+
+    part[z, other_rows, first:width] = (
+        part[z, other_rows, first:width].astype(jnp.float32)
+        + brecv[z].astype(jnp.float32)
+        + brecv[owners].astype(jnp.float32)
+    ).astype(jnp.bfloat16)
+    last_copy().start()
+
+    def finish(k, span, extra):
+        out_ref[lines(k), span] = (
+            xbuf[lines(k), span].astype(jnp.float32)
+            + part[z, lines(k, y), span].astype(jnp.float32)
+            + zrecv[z, lines(k), span].astype(jnp.float32)
+            + zrecv[owners, lines(k), span].astype(jnp.float32)
+            + extra.astype(jnp.float32)
+        ).astype(jnp.bfloat16)
+
     for k in range(chunks):
         y_copy(z, k).wait_recv()
-        total = (
-            xbuf[lines(k)].astype(jnp.float32)
-            + part[z, lines(k, y)].astype(jnp.float32)
-            + yrecv[z, lines(k)].astype(jnp.float32)
-        )
-        hid_zero = jnp.zeros((CHUNK, width), jnp.bfloat16)
 
         @pl.when(has_left)
         def _():
             z_copy(z, z, k, right).wait_recv()
 
-        @pl.when(jnp.logical_not(has_left))
-        def _():
-            zrecv[z, lines(k)] = hid_zero
-
         @pl.when(has_right)
         def _():
             z_copy(z, owners, k, left).wait_recv()
 
-        @pl.when(jnp.logical_not(has_right))
-        def _():
-            zrecv[owners, lines(k)] = hid_zero
-
-        total = total + (
-            zrecv[z, lines(k)].astype(jnp.float32)
-            + zrecv[owners, lines(k)].astype(jnp.float32)
-        )
-        out_ref[lines(k)] = total.astype(jnp.bfloat16)
+        finish(k, slice(0, first), yrecv[z, lines(k)])
+    last_copy().wait_recv()
+    for k in range(chunks):
+        finish(k, slice(first, width), bown[lines(k)])
 
     for k in range(chunks):
         x_copy(k).wait_send()
     for i in range(3):
         w_copies(i)[1].wait_send()
+    last_copy().wait_send()
+    for k in range(chunks):
+        t_copy(z, k, t_y, across).wait_send()
 
     def settle(zs, carry):
+        @pl.when(jnp.logical_and(zs <= z, has_right))
+        def _():
+            b_copy(zs, b_right, right).wait_send()
+
+        @pl.when(jnp.logical_and(zs >= z, has_left))
+        def _():
+            b_copy(zs, b_left, left).wait_send()
+
+        @pl.when(zs != z)
+        def _():
+            c_copy(zs, zs, right).wait_send()
+            for k in range(chunks):
+                a_copy(zs, y, k).wait_send()
+
         for k in range(chunks):
-            t_copy(zs, k, t_y, across).wait_send()
             y_copy(zs, k).wait_send()
 
             @pl.when(jnp.logical_and(zs <= z, has_right))
@@ -386,6 +496,17 @@
         hidden = w_gate.shape[3]
         chunks = rows // CHUNK
         tall = 2 * rows
+        tiles = width // 128
+        beyond = 128 * max(1, tiles // (2 * (owners - 1)))
+        column = jnp.arange(PAD, dtype=jnp.int32) % owners
+        dense = jnp.sum(
+            jnp.where(
+                route_ids[0][:, :, None] == column[None, None, :],
+                route_weights[0][:, :, None],
+                0.0,
+            ),
+            axis=1,
+        )
         vmem = pl.BlockSpec(memory_space=pltpu.VMEM)
         hbm = pl.BlockSpec(memory_space=pl.ANY)
         dma = pltpu.SemaphoreType.DMA
@@ -393,7 +514,7 @@
         out = pl.pallas_call(
             functools.partial(kernel, sizes),
             out_shape=jax.ShapeDtypeStruct((rows, width), jnp.bfloat16),
-            in_specs=[hbm, vmem, vmem, vmem, hbm, hbm, hbm],
+            in_specs=[hbm, vmem, vmem, hbm, hbm, hbm],
             out_specs=vmem,
             scratch_shapes=[
                 pltpu.VMEM((rows, width), jnp.bfloat16),
@@ -403,7 +524,7 @@
                 pltpu.VMEM((CORES, hidden, width), jnp.bfloat16),
                 pltpu.VMEM((tall, CORES * hidden), jnp.bfloat16),
                 pltpu.VMEM((owners, tall, width), jnp.bfloat16),
-                pltpu.VMEM((owners, rows, width), jnp.bfloat16),
+                pltpu.VMEM((owners, rows, width - beyond), jnp.bfloat16),
                 pltpu.VMEM((owners + 1, rows, width), jnp.bfloat16),
                 dma((chunks,)),
                 dma((chunks,)),
@@ -418,6 +539,14 @@
                 dma((owners, chunks)),
                 dma((owners, chunks)),
                 dma((owners + 1, chunks)),
+                pltpu.VMEM((owners + 1, rows, beyond), jnp.bfloat16),
+                pltpu.VMEM((rows, beyond), jnp.bfloat16),
+                dma((owners,)),
+                dma((owners,)),
+                dma((owners,)),
+                dma((owners,)),
+                dma((owners + 1,)),
+                dma((2,)),
             ],
             compiler_params=pltpu.CompilerParams(
                 collective_id=0,
@@ -431,8 +560,7 @@
             ),
         )(
             slab[0],
-            route_ids[0],
-            route_weights[0],
+            dense,
             norm_gain,
             w_gate[0, 0],
             w_up[0, 0],

time: 143 us -> 135 us (0.944)
  Pallas kernels: 138 us -> 131 us
  local copies, waits for them, and re-layouts: 4.73 us -> 1.99 us
    pallas_call x1, Pallas kernels: 138 us -> 131 us  [local(): pl.pallas_call(functools.partial(kernel, sizes), out_shape=jax.ShapeDtype...]
    squeeze x2 -> x0, local copies, waits for them, and re-layouts: 2.74 us -> none  [the longest x1 1.37 us: local(): route_ids[0]]
where the time goes in v2:
time: 135 us
  Pallas kernels  131 us (97%)
  local copies, waits for them, and re-layouts  1.99 us (1%)
  other arithmetic  1.4 us (1%)
    pallas_call x1, Pallas kernels, local(): pl.pallas_call(functools.partial(kernel, sizes), out_shape=jax.ShapeDtype...  131 us

profile of v2, /device:TPU:0, one launch (start us, length us, event | category | flops | bytes accessed | tf_op | source)
XLA Modules:
  0.0 134.9 jit_solution(3026673472643259314)
XLA Ops:
  0.0 1.4 %select_reduce_fusion.dense_ref = f32[48,128]{1,0:T(8,128)} fusion(f32[48,2]{0,1:T(2,128)} %bitcast.8, s32[128]{0:T(128)S(1)} %and_select_fusion, s32[48,2]{0,1:T(2,128)} %bitcast.9), kind=kLoop, calls=%fused_computation | loop fusion | flops 30720 | bytes 25856 | tf_op jit(solution)/shard_map/reduce_sum | solution.py:502
  1.4 131.5 %shard_map.73 = bf16[48,7168]{1,0:T(8,128)(2,1)} custom-call(bf16[48,7168]{1,0:T(8,128)(2,1)} %bitcast.13, f32[48,128]{1,0:T(8,128)} %select_reduce_fusion.dense_ref, f32[1,7168]{1,0:T(1,128)} %gain_ref.1, bf16[7168,256]{1,0:T(8,128)(2,1)} %bitcast.10, bf16[7168,256]{1,0:T(8,128)(2,1)} %bitcast.11, bf16[256,7168]{1,0:T(8,128)(2,1)} %bitcast.12), custom_call_target="tpu_custom_call" | custom-call | flops 8455716864 | bytes 22020096 | tf_op jit(solution)/shard_map/pallas_call | solution.py:514
  132.9 2.0 %copy.11 = bf16[1,48,7168]{2,1,0:T(8,128)(2,1)} copy(bf16[1,48,7168]{2,1,0:T(8,128)(2,1)} %bitcast.7) | data formatting | bytes 1376256
  (1 shorter events, 0.0 us)

commit v3 on v2

--- a/solution.py
+++ b/solution.py
@@ -185,31 +185,45 @@
         t_arrived(z, other_y, k).wait_recv()
     b_spread(z, has_right, has_left)
 
+    near = 1 - 2 * ((2 * z) // owners)
+
     def at(j):
-        return z + ((j + 1) // 2) * (1 - 2 * lax.rem(j, 2))
+        return z + ((j + 1) // 2) * (1 - 2 * lax.rem(j, 2)) * near
+
+    def outside_in(i):
+        return z - (owners - 1 - i // 2) * (1 - 2 * lax.rem(i, 2)) * near
 
     def inside(zs):
         return jnp.logical_and(zs >= 0, zs < owners)
 
-    def forward(zs):
+    def forward(sides):
         for k in range(chunks):
-            t_arrived(zs, y, k).wait_recv()
-
-            @pl.when(jnp.logical_and(zs < z, has_right))
-            def _():
-                t_copy(zs, k, t_right, right).start()
-
-            @pl.when(jnp.logical_and(zs > z, has_left))
-            def _():
-                t_copy(zs, k, t_left, left).start()
-
-            a_copy(zs, y, k).start()
-        b_copy(zs, b_right, right).wait_recv()
-        b_spread(
-            zs,
-            jnp.logical_and(zs < z, has_right),
-            jnp.logical_and(zs > z, has_left),
-        )
+            for zs in sides:
+
+                @pl.when(inside(zs))
+                def _():
+                    t_arrived(zs, y, k).wait_recv()
+
+                    @pl.when(jnp.logical_and(zs < z, has_right))
+                    def _():
+                        t_copy(zs, k, t_right, right).start()
+
+                    @pl.when(jnp.logical_and(zs > z, has_left))
+                    def _():
+                        t_copy(zs, k, t_left, left).start()
+
+                    a_copy(zs, y, k).start()
+
+        for zs in sides:
+
+            @pl.when(inside(zs))
+            def _():
+                b_copy(zs, b_right, right).wait_recv()
+                b_spread(
+                    zs,
+                    jnp.logical_and(zs < z, has_right),
+                    jnp.logical_and(zs > z, has_left),
+                )
 
     tall = 2 * rows
     hidden_width = wgs.shape[2]
@@ -256,11 +270,9 @@
         lax.fori_loop(0, width // tile, down, 0)
 
     def gather_step(j, carry):
-        zs = at(j)
-
-        @pl.when(jnp.logical_and(j < 2 * owners - 1, inside(zs)))
-        def _():
-            forward(zs)
+        @pl.when(jnp.logical_and(lax.rem(j, 2) == 1, j < 2 * owners - 1))
+        def _():
+            forward((at(j), at(j + 1)))
 
         before = at(j - 2)
 
@@ -322,7 +334,7 @@
         )
 
     def send_y(i, carry):
-        zs = at(2 * owners - 2 - i)
+        zs = outside_in(i)
 
         @pl.when(inside(zs))
         def _():
@@ -334,7 +346,7 @@
     lax.fori_loop(0, 2 * owners - 1, send_y, 0)
 
     def reduce_step(i, carry):
-        zs = at(2 * owners - 2 - i)
+        zs = outside_in(i)
 
         @pl.when(inside(zs))
         def _():
@@ -497,7 +509,7 @@
         chunks = rows // CHUNK
         tall = 2 * rows
         tiles = width // 128
-        beyond = 128 * max(1, tiles // (2 * (owners - 1)))
+        beyond = 128 * max(1, tiles // (2 * owners))
         column = jnp.arange(PAD, dtype=jnp.int32) % owners
         dense = jnp.sum(
             jnp.where(

time: 135 us -> 134 us (level)
  no operation moved by 1% of the time
where the time goes in v3:
time: 134 us
  Pallas kernels  130 us (97%)
  local copies, waits for them, and re-layouts  1.99 us (1%)
  other arithmetic  1.4 us (1%)
    pallas_call x1, Pallas kernels, local(): pl.pallas_call(functools.partial(kernel, sizes), out_shape=jax.ShapeDtype...  130 us

profile of v3, /device:TPU:0, one launch (start us, length us, event | category | flops | bytes accessed | tf_op | source)
XLA Modules:
  0.0 133.6 jit_solution(18207623545326450246)
XLA Ops:
  0.0 1.4 %select_reduce_fusion.dense_ref = f32[48,128]{1,0:T(8,128)} fusion(f32[48,2]{0,1:T(2,128)} %bitcast.8, s32[128]{0:T(128)S(1)} %and_select_fusion, s32[48,2]{0,1:T(2,128)} %bitcast.9), kind=kLoop, calls=%fused_computation | loop fusion | flops 30720 | bytes 25856 | tf_op jit(solution)/shard_map/reduce_sum | solution.py:514
  1.4 130.2 %shard_map.73 = bf16[48,7168]{1,0:T(8,128)(2,1)} custom-call(bf16[48,7168]{1,0:T(8,128)(2,1)} %bitcast.13, f32[48,128]{1,0:T(8,128)} %select_reduce_fusion.dense_ref, f32[1,7168]{1,0:T(1,128)} %gain_ref.1, bf16[7168,256]{1,0:T(8,128)(2,1)} %bitcast.10, bf16[7168,256]{1,0:T(8,128)(2,1)} %bitcast.11, bf16[256,7168]{1,0:T(8,128)(2,1)} %bitcast.12), custom_call_target="tpu_custom_call" | custom-call | flops 8455716864 | bytes 22020096 | tf_op jit(solution)/shard_map/pallas_call | solution.py:526
  131.6 2.0 %copy.11 = bf16[1,48,7168]{2,1,0:T(8,128)(2,1)} copy(bf16[1,48,7168]{2,1,0:T(8,128)(2,1)} %bitcast.7) | data formatting | bytes 1376256
  (1 shorter events, 0.0 us)
